TPU v7x, 512 devices: a whole 4x8x8 slice. The times are simulated.
512 devices in a mesh: region: 32 (over x, z), mp: 16 (over y, core).
Axes of the slice: x: 4, y: 8, z: 8, core: 2. Of those that a mesh axis runs over, the one named last changes fastest.
Arguments:
- tokens: bfloat16 [32768, 1024], P('region', 'mp'), may hold values from -6 to 6
- cotangent: bfloat16 [32768, 1024], P('region', 'mp'), may hold values from -6 to 6
- gain: float32 [1024], replicated, may hold values from 0.1 to 1.9
- w_up: bfloat16 [1024, 4096], P(None, 'mp'), may hold values from -0.1875 to 0.1875
- w_down: bfloat16 [4096, 1024], P('mp'), may hold values from -0.09375 to 0.09375
- counts: int32 [128], P('region'), may hold values from 16 to 256, as said below
Outputs:
- d_tokens: bfloat16 [32768, 1024], P('region', 'mp')
- d_up: float32 [1024, 4096], P('region', 'mp')
- d_down: float32 [4096, 1024], P('mp', 'region')
- d_gain: float32 [1024], P('mp')
Inputs may be any that keep to these rules, and one draw needn't show every extreme that they name: `counts`: each count is 16 times 1 + 3k for a whole k. Every group of 16 consecutive regions holds 1984 tokens, so all regions hold 15872 tokens together. The 4 regions of one owner hold at most 1024 tokens, and some owner holds exactly 1024 in every draw.
All inputs are finite; a program needn't handle non-finite values.
Results may differ from a plain program's by a relative error of at most 0.015.
Values may be sent and summed in bfloat16 or wider, within the bound.
A program may use at most 64 MiB of HBM per device.

v0:
```python
import math
import jax
import jax.numpy as jnp
from jax import lax
from jax.sharding import Mesh
from jax.sharding import PartitionSpec as P

BAL = 496
MP = ("mp_0", "mp_1")
EPSILON = 1e-05


def turned_gather(arrays, axis, dims):
    turned = [jnp.moveaxis(a, dim, 0) for a, dim in zip(arrays, dims)]
    widths = [t[0].size for t in turned]
    both = jnp.concatenate([t.reshape(-1, w) for t, w in zip(turned, widths)], axis=1)
    whole = lax.all_gather(both, axis, axis=0, tiled=True)
    blocks = jnp.split(whole, [sum(widths[:k]) for k in range(1, len(widths))], axis=1)
    return tuple(
        (
            jnp.moveaxis(b.reshape(-1, *t.shape[1:]), 0, dim)
            for b, t, dim in zip(blocks, turned, dims)
        )
    )


def split_up(value, dim, length):
    lengths = value.shape
    blocks = value.reshape(*lengths[:dim], length, lengths[dim] // length, *lengths[dim + 1 :])
    return jnp.moveaxis(blocks, dim, 0)


def sum_by_chip(value, chips, core, dim):
    sizes = (lax.axis_size(chips), lax.axis_size(core))
    blocks = split_up(value, dim, sizes[0] * sizes[1])
    inside = blocks.shape[1:]
    blocks = blocks.reshape(*sizes, *inside).swapaxes(0, 1).reshape(-1, *inside)
    blocks = lax.psum_scatter(blocks, core, scatter_dimension=0, tiled=True)
    return lax.psum_scatter(blocks, chips, scatter_dimension=0, tiled=True)[0]


def from_everyone(value, axis):
    length = lax.axis_size(axis)
    return lax.all_to_all(
        jnp.broadcast_to(value[None], (length, *value.shape)), axis, 0, 0, tiled=True
    )


def taken_together(value, axis):
    return from_everyone(value, axis).sum(axis=0)


def sum_at_owner(value, axis, dim):
    length = lax.axis_size(axis)
    blocks = lax.all_to_all(split_up(value, dim, length), axis, 0, 0, tiled=True)
    return jnp.sum(blocks.astype(jnp.float32), axis=0)


def gelu_tanh(inputs):
    return jax.nn.gelu(inputs, approximate=True)


def backward(rows_x, rows_dy, live_rows, gain, w_up, w_down, grad_scale):
    whole_x, whole_dy = turned_gather((rows_x, rows_dy), MP, (1, 1))
    share_width = rows_x.shape[1]
    feature_count = whole_x.shape[1]
    whole_float = whole_x.astype(jnp.float32)
    inv_rms = lax.rsqrt(jnp.mean(whole_float * whole_float, axis=1) + EPSILON)
    normed = (whole_float * inv_rms[:, None] * gain).astype(jnp.bfloat16)
    hidden = jnp.dot(normed, w_up, preferred_element_type=jnp.float32)
    activated, gelu_back = jax.vjp(gelu_tanh, hidden)
    act_rows = (activated * live_rows[:, None]).astype(jnp.bfloat16)
    d_act = lax.dot_general(
        whole_dy, w_down, (((1,), (1,)), ((), ())), preferred_element_type=jnp.float32
    )
    d_hidden = (gelu_back(d_act)[0] * live_rows[:, None]).astype(jnp.bfloat16)
    partial_term = lax.dot_general(
        d_hidden, w_up, (((1,), (1,)), ((), ())), preferred_element_type=jnp.float32
    )
    d_normed = sum_by_chip(partial_term.astype(jnp.bfloat16), "mp_0", "mp_1", 1).astype(jnp.float32)
    offset = lax.axis_index(MP) * share_width
    gain_part = lax.dynamic_slice_in_dim(gain, offset, share_width)
    x_part = rows_x.astype(jnp.float32)
    weighted = gain_part * d_normed
    row_dot = taken_together(jnp.sum(weighted * x_part, axis=1), MP)
    cubed = inv_rms * inv_rms * inv_rms
    d_rows = (
        rows_dy.astype(jnp.float32)
        + weighted * inv_rms[:, None]
        - x_part * (row_dot * cubed / feature_count)[:, None]
    )
    d_rows = (d_rows * live_rows[:, None]).astype(jnp.bfloat16)
    gain_term = jnp.sum(d_normed * x_part * (inv_rms * live_rows)[:, None], axis=0) * grad_scale
    up_term = lax.dot_general(
        normed, d_hidden, (((0,), (0,)), ((), ())), preferred_element_type=jnp.float32
    )
    down_term = lax.dot_general(
        whole_dy, act_rows, (((0,), (0,)), ((), ())), preferred_element_type=jnp.float32
    )
    grads = jnp.stack([up_term, down_term]) * grad_scale
    grads_part = sum_at_owner(grads.astype(jnp.bfloat16), "region", 1)
    gain_grad = taken_together(gain_term, "region")
    return (d_rows, grads_part, gain_grad)


def on_device(tokens, cotangent, gain, w_up, w_down, counts):
    regions_n = lax.axis_size("region")
    rows_cap = tokens.shape[0]
    grad_scale = 1.0 / math.sqrt(BAL * regions_n)
    own_load = jnp.sum(counts)
    own_rows = jnp.arange(rows_cap, dtype=jnp.int32)
    live_rows = (own_rows < own_load).astype(jnp.float32)
    d_tokens, grads_part, gain_grad = backward(
        tokens, cotangent, live_rows, gain, w_up, w_down, grad_scale
    )
    return (d_tokens, grads_part[0], grads_part[1].T, gain_grad)


def solution(mesh):
    torus = Mesh(mesh.devices.reshape(mesh.shape["region"], 8, 2), ("region", "mp_0", "mp_1"))
    in_specs = (P("region", MP), P("region", MP), P(), P(None, MP), P(MP, None), P("region"))
    out_specs = (P("region", MP), P("region", MP), P(MP, "region"), P(MP))
    return jax.shard_map(
        on_device, mesh=torus, in_specs=in_specs, out_specs=out_specs, check_vma=False
    )
```

profile of v0, /device:TPU:1, one launch (start us, length us, event | category | flops | bytes accessed | tf_op | source)
XLA Modules:
  0.0 175.7 jit_solution(16805085722291044228)
XLA Ops:
  7.2 0.0 copy-start
  7.2 0.0 all-gather.2.cloned.1.call-start
  7.2 1.7 pad_maximum_fusion
  8.9 0.0 all-gather.2.cloned.1.call-update
  9.0 0.0 reduce-scatter.3.cloned.1.call-start
  9.0 1.3 reduce_sum.64
  10.3 0.6 fusion.39
  11.0 49.7 %all-gather.2.cloned.1.call-done = bf16[1024,2048]{1,0:T(8,128)(2,1)} async-done(((bf16[64,2048]{1,0:T(8,128)(2,1)}), bf16[1024,2048]{1,0:T(8,128)(2,1)}) %all-gather.2.cloned.1.call-update) | async-done | bytes 4194320 | tf_op jit(solution)/shard_map/all_gather | solution.py:17
  60.6 2.1 %fusion = f32[1024]{0:T(1024)S(1)} fusion(bf16[1024,2048]{1,0:T(8,128)(2,1)} %all-gather.2.cloned.1.call-done), kind=kLoop, calls=%fused_computation.2 | loop fusion | flops 3144704 | bytes 2101248 | tf_op jit(solution)/shard_map/reduce_sum | solution.py:68
  62.7 0.6 fusion.38
  63.4 0.0 copy-done
  63.4 0.0 copy-start.2
  63.4 0.0 copy-start.4
  63.4 2.7 %fusion.26 = f32[1024,256]{1,0:T(8,128)S(1)} fusion(bf16[1024,256]{1,0:T(8,128)(2,1)S(1)} %copy-done, f32[1024]{0:T(1024)} %param.8, f32[1024]{0:T(1024)S(1)} %get-tuple-element.9, bf16[1024,2048]{1,0:T(8,128)(2,1)} %all-gather.2.cloned.1.call-done), kind=kOutput, calls=%fused_computation.34 | convolution fusion | flops 541065216 | bytes 3678208 | tf_op jit(solution)/shard_map/dot_general | solution.py:70
  66.1 0.1 copy-done.2
  66.2 0.1 copy-done.4
  66.3 1.3 fusion.15
  67.7 0.7 convolution_convert_fusion
  68.4 1.5 copy.17
  69.9 0.0 reduce-scatter.3.cloned.1.call-update
  69.9 0.0 copy-start.5
  70.0 0.0 reduce-scatter.5.cloned.1.call-start
  70.0 2.5 %fusion.4 = f32[1024,256]{1,0:T(8,128)S(1)} fusion(bf16[1024,2048]{1,0:T(8,128)(2,1)} %all-gather.2.cloned.1.call-done, f32[1024,256]{1,0:T(8,128)S(1)} %fusion.26, f32[1024]{0:T(1024)S(1)} %fusion.39), kind=kOutput, calls=%fused_computation.9 | convolution fusion | flops 539492352 | bytes 4198400 | tf_op jit(solution)/shard_map/dot_general | solution.py:97
  72.5 15.5 %reduce-scatter.3.cloned.1.call-done = bf16[8,1024,64]{1,2,0:T(8,128)(2,1)} async-done(((bf16[16,1024,64]{1,2,0:T(8,128)(2,1)}), bf16[8,1024,64]{1,2,0:T(8,128)(2,1)}) %reduce-scatter.3.cloned.1.call-update) | async-done | bytes 1048592 | tf_op jit(solution)/shard_map/reduce_scatter | solution.py:38
  87.9 0.0 reduce-scatter.5.cloned.1.call-update
  87.9 0.0 copy-done.5
  88.0 2.4 %fusion.24 = f32[1024,256]{1,0:T(8,128)S(1)} fusion(bf16[1024,256]{1,0:T(8,128)(2,1)S(1)} %fusion.15, f32[1024]{0:T(1024)S(1)} %copy-done.5, f32[1024]{0:T(1024)S(1)} %get-tuple-element.9, bf16[1024,2048]{1,0:T(8,128)(2,1)} %all-gather.2.cloned.1.call-done), kind=kOutput, calls=%fused_computation.33 | convolution fusion | flops 541065216 | bytes 3678208 | tf_op jit(solution)/shard_map/dot_general | solution.py:94
  90.3 0.0 copy-start.1
  90.3 0.0 copy-start.3
  90.3 1.3 fusion.16
  91.6 9.0 %all-to-all-start.1 = ((bf16[32,2,32,256]{3,2,1,0:T(8,128)(2,1)}), bf16[32,2,32,256]{3,2,1,0:T(8,128)(2,1)S(1)}, u32[]{:S(2)}, u32[]{:S(2)}) async-start(bf16[32,2,32,256]{3,2,1,0:T(8,128)(2,1)} %fusion.16), calls=%async_computation.3 | async-start | bytes 2097152 | tf_op jit(solution)/shard_map/all_to_all | solution.py:55
  100.7 0.1 dynamic_slice.3
  100.7 27.4 %reduce-scatter.5.cloned.1.call-done = bf16[1,1024,64]{1,2,0:T(8,128)(2,1)} async-done(((bf16[8,1024,64]{1,2,0:T(8,128)(2,1)}), bf16[1,1024,64]{1,2,0:T(8,128)(2,1)}) %reduce-scatter.5.cloned.1.call-update) | async-done | bytes 131088 | tf_op jit(solution)/shard_map/reduce_scatter | solution.py:39
  128.1 0.0 copy-done.1
  128.1 1.1 fusion.35
  129.2 0.0 all-to-all-done.1
  129.3 0.6 broadcast_in_dim.5
  129.9 9.8 %all-to-all-start.2 = ((f32[32,1,64]{2,1,0:T(1,128)}), f32[32,1,64]{2,1,0:T(1,128)S(1)}, u32[]{:S(2)}, u32[]{:S(2)}) async-start(f32[32,1,64]{2,1,0:T(1,128)} %broadcast_in_dim.5), calls=%async_computation.4 | async-start | bytes 32768 | tf_op jit(solution)/shard_map/all_to_all | solution.py:44
  139.7 0.2 convert_reduce_fusion
  139.8 8.4 %all-to-all-done.2 = f32[32,1,64]{2,1,0:T(1,128)S(1)} async-done(((f32[32,1,64]{2,1,0:T(1,128)}), f32[32,1,64]{2,1,0:T(1,128)S(1)}, u32[]{:S(2)}, u32[]{:S(2)}) %all-to-all-start.2) | async-done | bytes 8224 | tf_op jit(solution)/shard_map/all_to_all | solution.py:44
  148.2 0.7 broadcast_in_dim.4
  148.9 10.6 %all-to-all-start = ((f32[16,1,1024]{2,1,0:T(1,128)}), f32[16,1,1024]{2,1,0:T(1,128)S(1)}, u32[]{:S(2)}, u32[]{:S(2)}) async-start(f32[16,1,1024]{2,1,0:T(1,128)} %broadcast_in_dim.4), calls=%async_computation.2 | async-start | bytes 131072 | tf_op jit(solution)/shard_map/all_to_all | solution.py:44
  159.6 0.6 slice_bitcast_fusion
  160.2 0.5 reduce_sum.69
  160.7 6.6 %all-to-all-done = f32[16,1,1024]{2,1,0:T(1,128)S(1)} async-done(((f32[16,1,1024]{2,1,0:T(1,128)}), f32[16,1,1024]{2,1,0:T(1,128)S(1)}, u32[]{:S(2)}, u32[]{:S(2)}) %all-to-all-start) | async-done | bytes 65568 | tf_op jit(solution)/shard_map/all_to_all | solution.py:44
  167.4 0.1 reduce_sum.66
  167.4 0.0 copy-done.3
  167.4 1.7 fusion.32
  (2 shorter events, 0.0 us)
Async XLA Ops:
  7.2 56.2 %copy-start = (bf16[1024,256]{1,0:T(8,128)(2,1)S(1)}, bf16[1024,256]{1,0:T(8,128)(2,1)}, u32[]{:S(2)}) copy-start(bf16[1024,256]{1,0:T(8,128)(2,1)} %param.9) | copy-start | bytes 1572868
  7.2 53.5 %all-gather.2.cloned.1.call-start = ((), (), s32[]{:S(2)}) async-start(), calls=%async_computation.5 | async-start | bytes 4456448 | tf_op jit(solution)/shard_map/all_gather | solution.py:17
  9.0 78.9 %reduce-scatter.3.cloned.1.call-start = ((), (), s32[]{:S(2)}) async-start(), calls=%async_computation.6 | async-start | bytes 3145728 | tf_op jit(solution)/shard_map/reduce_scatter | solution.py:38
  63.4 2.8 %copy-start.2 = (bf16[1024,2048]{1,0:T(8,128)(2,1)S(1)}, bf16[1024,2048]{1,0:T(8,128)(2,1)}, u32[]{:S(2)}) copy-start(bf16[1024,2048]{1,0:T(8,128)(2,1)} %all-gather.2.cloned.1.call-done) | copy-start | bytes 12582916
  63.4 2.9 %copy-start.4 = (bf16[256,1024]{1,0:T(8,128)(2,1)S(1)}, bf16[256,1024]{1,0:T(8,128)(2,1)}, u32[]{:S(2)}) copy-start(bf16[256,1024]{1,0:T(8,128)(2,1)} %param.10) | copy-start | bytes 1572868
  69.9 18.0 %copy-start.5 = (f32[1024]{0:T(1024)S(1)}, f32[1024]{0:T(1024)}, u32[]{:S(2)}) copy-start(f32[1024]{0:T(1024)} %param.8) | copy-start | bytes 12292
  70.0 58.1 %reduce-scatter.5.cloned.1.call-start = ((), (), s32[]{:S(2)}) async-start(), calls=%async_computation.7 | async-start | bytes 1179648 | tf_op jit(solution)/shard_map/reduce_scatter | solution.py:39
  90.3 37.8 %copy-start.1 = (bf16[1024,64]{0,1:T(8,128)(2,1)S(1)}, bf16[1024,64]{0,1:T(8,128)(2,1)}, u32[]{:S(2)}) copy-start(bf16[1024,64]{0,1:T(8,128)(2,1)} %param.6) | copy-start | bytes 393220
  90.3 77.1 %copy-start.3 = (bf16[1024,64]{0,1:T(8,128)(2,1)S(1)}, bf16[1024,64]{0,1:T(8,128)(2,1)}, u32[]{:S(2)}) copy-start(bf16[1024,64]{0,1:T(8,128)(2,1)} %param.7) | copy-start | bytes 393220
  91.6 37.6 %all-to-all-start.1 = ((bf16[32,2,32,256]{3,2,1,0:T(8,128)(2,1)}), bf16[32,2,32,256]{3,2,1,0:T(8,128)(2,1)S(1)}, u32[]{:S(2)}, u32[]{:S(2)}) async-start(bf16[32,2,32,256]{3,2,1,0:T(8,128)(2,1)} %fusion.16), calls=%async_computation.3 | async-start | bytes 2097152 | tf_op jit(solution)/shard_map/all_to_all | solution.py:55
  129.9 18.4 %all-to-all-start.2 = ((f32[32,1,64]{2,1,0:T(1,128)}), f32[32,1,64]{2,1,0:T(1,128)S(1)}, u32[]{:S(2)}, u32[]{:S(2)}) async-start(f32[32,1,64]{2,1,0:T(1,128)} %broadcast_in_dim.5), calls=%async_computation.4 | async-start | bytes 32768 | tf_op jit(solution)/shard_map/all_to_all | solution.py:44
  148.9 18.5 %all-to-all-start = ((f32[16,1,1024]{2,1,0:T(1,128)}), f32[16,1,1024]{2,1,0:T(1,128)S(1)}, u32[]{:S(2)}, u32[]{:S(2)}) async-start(f32[16,1,1024]{2,1,0:T(1,128)} %broadcast_in_dim.4), calls=%async_computation.2 | async-start | bytes 131072 | tf_op jit(solution)/shard_map/all_to_all | solution.py:44
Sparse Core Ops, SparseCore 0:
  10.1 50.4 all-gather.1
  70.1 17.8 reduce-scatter.2
  91.0 37.0 reduce-scatter.4
where the time goes:
time: 176 us
  waiting for transfers between devices  108 us (61%)
  starting transfers between devices  29.6 us (17%)
  between operations  13.9 us (8%)
  other arithmetic  11.2 us (6%)
  matrix products  9.63 us (5%)
  local copies, waits for them, and re-layouts  3.7 us (2%)
    all_gather x1, waiting for transfers between devices, turned_gather(): whole = lax.all_gather(both, axis, axis=0, tiled=True)  49.7 us
    reduce_scatter x1, waiting for transfers between devices, sum_by_chip(): return lax.psum_scatter(blocks, chips, scatter_dimension=0, tiled=True)[0]  27.4 us
    all_to_all x2, starting transfers between devices, from_everyone(): lax.all_to_all(jnp.broadcast_to(value[None], (length, *value.shape)), axi...  20.4 us
    reduce_scatter x1, waiting for transfers between devices, sum_by_chip(): blocks = lax.psum_scatter(blocks, core, scatter_dimension=0, tiled=True)  15.5 us
    all_to_all x2, waiting for transfers between devices, from_everyone(): lax.all_to_all(jnp.broadcast_to(value[None], (length, *value.shape)), axi...  15 us
    all_to_all x1, starting transfers between devices, sum_at_owner(): lax.all_to_all(split_up(value, dim, length), axis, 0, 0, tiled=True)  9.03 us
  transfers between devices with their start and end apart: 6, of which 5 were waited for; matrix products, arithmetic and copies ran while one was open for 6% of the time, Pallas kernels for 0%

commit v1 on v0

--- a/solution.py
+++ b/solution.py
@@ -14,7 +14,9 @@
     turned = [jnp.moveaxis(a, dim, 0) for a, dim in zip(arrays, dims)]
     widths = [t[0].size for t in turned]
     both = jnp.concatenate([t.reshape(-1, w) for t, w in zip(turned, widths)], axis=1)
-    whole = lax.all_gather(both, axis, axis=0, tiled=True)
+    whole = jnp.concatenate(
+        lax.all_to_all(jnp.stack([both] * lax.axis_size(axis)), axis, 0, 0), axis=0
+    )
     blocks = jnp.split(whole, [sum(widths[:k]) for k in range(1, len(widths))], axis=1)
     return tuple(
         (

time: 176 us -> 234 us (1.33)
  waiting for transfers between devices: 108 us -> 151 us
  starting transfers between devices: 29.6 us -> 40.9 us
    all_to_all x0 -> x1, waiting for transfers between devices: none -> 92.3 us  [turned_gather(): lax.all_to_all(jnp.stack([both] * lax.axis_size(axis)), axis, 0, 0)]
    all_gather x1 -> x0, waiting for transfers between devices: 49.7 us -> none  [turned_gather(): whole = lax.all_gather(both, axis, axis=0, tiled=True)]
    all_to_all x0 -> x1, starting transfers between devices: none -> 11.3 us  [turned_gather(): lax.all_to_all(jnp.stack([both] * lax.axis_size(axis)), axis, 0, 0)]
    another operation x0 -> x1, local copies, waits for them, and re-layouts: none -> 2.49 us  [turned_gather(): jnp.stack([both] * lax.axis_size(axis))]
  transfers between devices with their start and end apart: 6 -> 6, of which waited for: 5 -> 5; matrix products, arithmetic and copies ran while one was open for 6% -> 4% of each run, Pallas kernels for 0% -> 0%
where the time goes in v1:
time: 234 us; the launch traced here: 233 us
  waiting for transfers between devices  151 us (65%)
  starting transfers between devices  40.9 us (17%)
  between operations  14.2 us (6%)
  matrix products  11.1 us (5%)
  other arithmetic  9.9 us (4%)
  local copies, waits for them, and re-layouts  6.01 us (3%)
    all_to_all x1, waiting for transfers between devices, turned_gather(): lax.all_to_all(jnp.stack([both] * lax.axis_size(axis)), axis, 0, 0)  92.3 us
    reduce_scatter x1, waiting for transfers between devices, sum_by_chip(): return lax.psum_scatter(blocks, chips, scatter_dimension=0, tiled=True)[0]  27.2 us
    all_to_all x2, starting transfers between devices, from_everyone(): lax.all_to_all(jnp.broadcast_to(value[None], (length, *value.shape)), axi...  20.5 us
    reduce_scatter x1, waiting for transfers between devices, sum_by_chip(): blocks = lax.psum_scatter(blocks, core, scatter_dimension=0, tiled=True)  16.5 us
    all_to_all x2, waiting for transfers between devices, from_everyone(): lax.all_to_all(jnp.broadcast_to(value[None], (length, *value.shape)), axi...  15 us
    all_to_all x1, starting transfers between devices, turned_gather(): lax.all_to_all(jnp.stack([both] * lax.axis_size(axis)), axis, 0, 0)  11.3 us
    all_to_all x1, starting transfers between devices, sum_at_owner(): lax.all_to_all(split_up(value, dim, length), axis, 0, 0, tiled=True)  9.04 us
  transfers between devices with their start and end apart: 6, of which 5 were waited for; matrix products, arithmetic and copies ran while one was open for 4% of the time, Pallas kernels for 0%

profile of v1, /device:TPU:1, one launch (start us, length us, event | category | flops | bytes accessed | tf_op | source)
XLA Modules:
  0.0 233.3 jit_solution(2197092381190453099)
XLA Ops:
  7.2 0.0 copy-start
  7.2 1.0 pad_maximum_fusion
  8.2 2.5 %stack.8 = bf16[16,64,2048]{2,1,0:T(8,128)(2,1)} broadcast(bf16[64,2048]{1,0:T(8,128)(2,1)S(1)} %pad_maximum_fusion), dimensions={1,2} | broadcast | bytes 4456448 | tf_op jit(solution)/shard_map/stack | solution.py:18
  10.7 0.0 copy-start.5
  10.7 0.0 copy-start.4
  10.7 11.3 %all-to-all-start = ((bf16[16,64,2048]{2,1,0:T(8,128)(2,1)}), bf16[16,64,2048]{2,1,0:T(8,128)(2,1)}, u32[]{:S(2)}, u32[]{:S(2)}) async-start(bf16[16,64,2048]{2,1,0:T(8,128)(2,1)} %stack.8), calls=%async_computation | async-start | bytes 8388608 | tf_op jit(solution)/shard_map/all_to_all | solution.py:18
  22.0 0.0 reduce-scatter.3.cloned.1.call-start
  22.0 0.0 copy-done.5
  22.1 0.6 reduce_sum.64
  22.7 0.6 fusion.39
  23.3 92.3 %all-to-all-done = bf16[16,64,2048]{2,1,0:T(8,128)(2,1)} async-done(((bf16[16,64,2048]{2,1,0:T(8,128)(2,1)}), bf16[16,64,2048]{2,1,0:T(8,128)(2,1)}, u32[]{:S(2)}, u32[]{:S(2)}) %all-to-all-start) | async-done | bytes 4194336 | tf_op jit(solution)/shard_map/all_to_all | solution.py:18
  115.7 2.1 fusion
  117.8 0.6 fusion.38
  118.4 0.0 copy-done
  118.4 0.0 copy-done.4
  118.4 0.0 copy-start.3
  118.4 2.6 %fusion.26 = f32[1024,256]{1,0:T(8,128)S(1)} fusion(bf16[1024,256]{1,0:T(8,128)(2,1)S(1)} %copy-done, f32[1024]{0:T(1024)S(1)} %copy-done.4, f32[1024]{0:T(1024)S(1)} %get-tuple-element.9, bf16[1024,2048]{1,0:T(8,128)(2,1)} %bitcast.2), kind=kOutput, calls=%fused_computation.34 | convolution fusion | flops 541065216 | bytes 3678208 | tf_op jit(solution)/shard_map/dot_general | solution.py:72
  121.1 0.0 copy-done.3
  121.1 2.9 %fusion.15 = bf16[1024,256]{1,0:T(8,128)(2,1)S(1)} fusion(f32[1024,256]{1,0:T(8,128)S(1)} %fusion.26, bf16[256,1024]{1,0:T(8,128)(2,1)S(1)} %copy-done.3, bf16[1024,2048]{1,0:T(8,128)(2,1)} %bitcast.2, f32[1024]{0:T(1024)S(1)} %fusion.39), kind=kOutput, calls=%fused_computation.22 | convolution fusion | flops 542375936 | bytes 4198400 | tf_op jit(solution)/shard_map/dot_general | solution.py:75
  124.0 0.7 convolution_convert_fusion
  124.7 1.5 copy.17
  126.2 0.0 reduce-scatter.3.cloned.1.call-update
  126.3 0.0 reduce-scatter.5.cloned.1.call-start
  126.3 2.5 %fusion.4 = f32[1024,256]{1,0:T(8,128)S(1)} fusion(bf16[1024,2048]{1,0:T(8,128)(2,1)} %bitcast.2, f32[1024,256]{1,0:T(8,128)S(1)} %fusion.26, f32[1024]{0:T(1024)S(1)} %fusion.39), kind=kOutput, calls=%fused_computation.9 | convolution fusion | flops 539492352 | bytes 4198400 | tf_op jit(solution)/shard_map/dot_general | solution.py:99
  128.8 16.5 %reduce-scatter.3.cloned.1.call-done = bf16[8,1024,64]{1,2,0:T(8,128)(2,1)} async-done(((bf16[16,1024,64]{1,2,0:T(8,128)(2,1)}), bf16[8,1024,64]{1,2,0:T(8,128)(2,1)}) %reduce-scatter.3.cloned.1.call-update) | async-done | bytes 1048592 | tf_op jit(solution)/shard_map/reduce_scatter | solution.py:40
  145.3 0.0 reduce-scatter.5.cloned.1.call-update
  145.3 2.3 %fusion.24 = f32[1024,256]{1,0:T(8,128)S(1)} fusion(bf16[1024,256]{1,0:T(8,128)(2,1)S(1)} %fusion.15, f32[1024]{0:T(1024)S(1)} %copy-done.4, f32[1024]{0:T(1024)S(1)} %get-tuple-element.9, bf16[1024,2048]{1,0:T(8,128)(2,1)} %bitcast.2), kind=kOutput, calls=%fused_computation.33 | convolution fusion | flops 541065216 | bytes 3678208 | tf_op jit(solution)/shard_map/dot_general | solution.py:96
  147.7 0.0 copy-start.1
  147.7 0.0 copy-start.2
  147.7 1.3 fusion.16
  149.0 9.0 %all-to-all-start.2 = ((bf16[32,2,32,256]{3,2,1,0:T(8,128)(2,1)}), bf16[32,2,32,256]{3,2,1,0:T(8,128)(2,1)S(1)}, u32[]{:S(2)}, u32[]{:S(2)}) async-start(bf16[32,2,32,256]{3,2,1,0:T(8,128)(2,1)} %fusion.16), calls=%async_computation.4 | async-start | bytes 2097152 | tf_op jit(solution)/shard_map/all_to_all | solution.py:57
  158.0 0.1 dynamic_slice.3
  158.1 27.2 %reduce-scatter.5.cloned.1.call-done = bf16[1,1024,64]{1,2,0:T(8,128)(2,1)} async-done(((bf16[8,1024,64]{1,2,0:T(8,128)(2,1)}), bf16[1,1024,64]{1,2,0:T(8,128)(2,1)}) %reduce-scatter.5.cloned.1.call-update) | async-done | bytes 131088 | tf_op jit(solution)/shard_map/reduce_scatter | solution.py:41
  185.3 0.0 copy-done.1
  185.3 1.1 fusion.35
  186.4 0.0 all-to-all-done.2
  186.4 0.6 broadcast_in_dim.5
  187.1 9.9 %all-to-all-start.3 = ((f32[32,1,64]{2,1,0:T(1,128)}), f32[32,1,64]{2,1,0:T(1,128)S(1)}, u32[]{:S(2)}, u32[]{:S(2)}) async-start(f32[32,1,64]{2,1,0:T(1,128)} %broadcast_in_dim.5), calls=%async_computation.5 | async-start | bytes 32768 | tf_op jit(solution)/shard_map/all_to_all | solution.py:46
  197.0 0.2 convert_reduce_fusion
  197.2 8.4 %all-to-all-done.3 = f32[32,1,64]{2,1,0:T(1,128)S(1)} async-done(((f32[32,1,64]{2,1,0:T(1,128)}), f32[32,1,64]{2,1,0:T(1,128)S(1)}, u32[]{:S(2)}, u32[]{:S(2)}) %all-to-all-start.3) | async-done | bytes 8224 | tf_op jit(solution)/shard_map/all_to_all | solution.py:46
  205.6 0.7 broadcast_in_dim.4
  206.2 10.6 %all-to-all-start.1 = ((f32[16,1,1024]{2,1,0:T(1,128)}), f32[16,1,1024]{2,1,0:T(1,128)S(1)}, u32[]{:S(2)}, u32[]{:S(2)}) async-start(f32[16,1,1024]{2,1,0:T(1,128)} %broadcast_in_dim.4), calls=%async_computation.3 | async-start | bytes 131072 | tf_op jit(solution)/shard_map/all_to_all | solution.py:46
  216.8 0.6 slice_bitcast_fusion
  217.5 0.5 reduce_sum.69
  218.0 6.6 %all-to-all-done.1 = f32[16,1,1024]{2,1,0:T(1,128)S(1)} async-done(((f32[16,1,1024]{2,1,0:T(1,128)}), f32[16,1,1024]{2,1,0:T(1,128)S(1)}, u32[]{:S(2)}, u32[]{:S(2)}) %all-to-all-start.1) | async-done | bytes 65568 | tf_op jit(solution)/shard_map/all_to_all | solution.py:46
  224.7 0.1 reduce_sum.66
  224.7 0.0 copy-done.2
  224.7 1.7 fusion.32
  (2 shorter events, 0.0 us)
Async XLA Ops:
  7.2 111.2 %copy-start = (bf16[1024,256]{1,0:T(8,128)(2,1)S(1)}, bf16[1024,256]{1,0:T(8,128)(2,1)}, u32[]{:S(2)}) copy-start(bf16[1024,256]{1,0:T(8,128)(2,1)} %param.9) | copy-start | bytes 1572868
  10.7 11.3 %copy-start.5 = (s32[4]{0:T(128)S(1)}, s32[4]{0:T(128)}, u32[]{:S(2)}) copy-start(s32[4]{0:T(128)} %param.11) | copy-start | bytes 52
  10.7 107.7 %copy-start.4 = (f32[1024]{0:T(1024)S(1)}, f32[1024]{0:T(1024)}, u32[]{:S(2)}) copy-start(f32[1024]{0:T(1024)} %param.8) | copy-start | bytes 12292
  10.7 105.0 %all-to-all-start = ((bf16[16,64,2048]{2,1,0:T(8,128)(2,1)}), bf16[16,64,2048]{2,1,0:T(8,128)(2,1)}, u32[]{:S(2)}, u32[]{:S(2)}) async-start(bf16[16,64,2048]{2,1,0:T(8,128)(2,1)} %stack.8), calls=%async_computation | async-start | bytes 8388608 | tf_op jit(solution)/shard_map/all_to_all | solution.py:18
  22.0 123.3 %reduce-scatter.3.cloned.1.call-start = ((), (), s32[]{:S(2)}) async-start(), calls=%async_computation.6 | async-start | bytes 3145728 | tf_op jit(solution)/shard_map/reduce_scatter | solution.py:40
  118.4 2.6 %copy-start.3 = (bf16[256,1024]{1,0:T(8,128)(2,1)S(1)}, bf16[256,1024]{1,0:T(8,128)(2,1)}, u32[]{:S(2)}) copy-start(bf16[256,1024]{1,0:T(8,128)(2,1)} %param.10) | copy-start | bytes 1572868
  126.3 59.0 %reduce-scatter.5.cloned.1.call-start = ((), (), s32[]{:S(2)}) async-start(), calls=%async_computation.7 | async-start | bytes 1179648 | tf_op jit(solution)/shard_map/reduce_scatter | solution.py:41
  147.7 37.6 %copy-start.1 = (bf16[1024,64]{0,1:T(8,128)(2,1)S(1)}, bf16[1024,64]{0,1:T(8,128)(2,1)}, u32[]{:S(2)}) copy-start(bf16[1024,64]{0,1:T(8,128)(2,1)} %param.6) | copy-start | bytes 393220
  147.7 77.0 %copy-start.2 = (bf16[1024,64]{0,1:T(8,128)(2,1)S(1)}, bf16[1024,64]{0,1:T(8,128)(2,1)}, u32[]{:S(2)}) copy-start(bf16[1024,64]{0,1:T(8,128)(2,1)} %param.7) | copy-start | bytes 393220
  149.0 37.5 %all-to-all-start.2 = ((bf16[32,2,32,256]{3,2,1,0:T(8,128)(2,1)}), bf16[32,2,32,256]{3,2,1,0:T(8,128)(2,1)S(1)}, u32[]{:S(2)}, u32[]{:S(2)}) async-start(bf16[32,2,32,256]{3,2,1,0:T(8,128)(2,1)} %fusion.16), calls=%async_computation.4 | async-start | bytes 2097152 | tf_op jit(solution)/shard_map/all_to_all | solution.py:57
  187.1 18.5 %all-to-all-start.3 = ((f32[32,1,64]{2,1,0:T(1,128)}), f32[32,1,64]{2,1,0:T(1,128)S(1)}, u32[]{:S(2)}, u32[]{:S(2)}) async-start(f32[32,1,64]{2,1,0:T(1,128)} %broadcast_in_dim.5), calls=%async_computation.5 | async-start | bytes 32768 | tf_op jit(solution)/shard_map/all_to_all | solution.py:46
  206.2 18.4 %all-to-all-start.1 = ((f32[16,1,1024]{2,1,0:T(1,128)}), f32[16,1,1024]{2,1,0:T(1,128)S(1)}, u32[]{:S(2)}, u32[]{:S(2)}) async-start(f32[16,1,1024]{2,1,0:T(1,128)} %broadcast_in_dim.4), calls=%async_computation.3 | async-start | bytes 131072 | tf_op jit(solution)/shard_map/all_to_all | solution.py:46
Sparse Core Ops, SparseCore 0:
  126.4 18.8 reduce-scatter.2
  148.3 36.9 reduce-scatter.4
